TPU v7x, 512 devices: a whole 4x4x16 slice. The times are simulated.
512 devices in a mesh: lo: 16 (over y, x), hi: 32 (over z, core).
Axes of the slice: x: 4, y: 4, z: 16, core: 2. Of those that a mesh axis runs over, the one named last changes fastest.
Arguments:
- points: bfloat16 [32, 16, 64, 4096], P('hi', 'lo'), may hold values from -6 to 6
- rhs: bfloat16 [32, 16, 4096, 128], P('hi', 'lo'), may hold values from -6 to 6
- order: int32 [32, 16, 4096], P('hi', 'lo'), may hold values from 0 to 4095, each once within a row
- anchors: bfloat16 [32, 16, 11, 64, 128], P('hi', 'lo'), may hold values from -6 to 6
- coupling: float32 [32, 16, 11, 128, 128], P('hi', 'lo'), may hold values from -18 to 18
Outputs:
- product: float32 [32, 16, 4096, 128], P('hi', 'lo')
All inputs are finite; a program needn't handle non-finite values.
Results may differ from a plain program's by a relative error of at most 0.0041.
Values sent between devices are 32-bit elements; how exact they have to be, the bound alone decides.
A program may use at most 128 MiB of HBM per device.

v0:
```python
import math

import jax
import jax.numpy as jnp
from jax import lax
from jax.sharding import PartitionSpec as P


def from_partner(block, axis, stride):
    count = lax.axis_size(axis)
    route = []
    for low in range(count):
        high = low | 1 << stride
        if high != low and high < count:
            route += [(low, high), (high, low)]
    return lax.ppermute(block, axis, route)


def kernel(left_pts, right_pts):
    cross_dot = lax.dot_general(
        left_pts, right_pts, (((0,), (0,)), ((), ())), preferred_element_type=jnp.float32
    )
    left_wide = left_pts.astype(jnp.float32)
    right_wide = right_pts.astype(jnp.float32)
    sq_dist = (
        jnp.sum(left_wide * left_wide, 0)[:, None]
        + jnp.sum(right_wide * right_wide, 0)[None, :]
        - 2.0 * cross_dot
    )
    return jnp.exp(sq_dist * (-2.0 / left_pts.shape[0]))


def far_basis(leaf_pts, anchor_set):
    emb_width = anchor_set.shape[1]
    far_sets = anchor_set.shape[0] - 2
    flat_anchors = jnp.transpose(anchor_set[2:], (1, 0, 2)).reshape(
        emb_width, far_sets * anchor_set.shape[2]
    )
    return kernel(leaf_pts, flat_anchors).astype(jnp.bfloat16)


def contract_rows(basis_block, row_block):
    return lax.dot_general(
        basis_block, row_block, (((0,), (0,)), ((), ())), preferred_element_type=jnp.float32
    )


def apply_device(leaf_pts, leaf_rows, anchor_set, core_set, sibling_coef, perm_rows, basis_far):
    pts_count = leaf_pts.shape[1]
    leaf_size = pts_count // 2
    far_sets = anchor_set.shape[0] - 2
    rank_size = anchor_set.shape[2]
    rhs_count = leaf_rows.shape[1]
    level_scale = jnp.array(
        [1.0 / math.sqrt(pts_count * 2.0**level) for level in range(far_sets)], jnp.float32
    )
    scaled = sibling_coef * level_scale[:, None, None]
    far_mix = jnp.einsum("lrs,lsn->lrn", core_set[2:], scaled, precision=lax.Precision.HIGHEST)
    far_mix = far_mix.astype(jnp.bfloat16).reshape(far_sets * rank_size, rhs_count)
    leaf_parts = []
    leaf_bases = []
    leaf_coefs = []
    for leaf_half in range(2):
        block_pts = leaf_pts[:, leaf_half * leaf_size : (leaf_half + 1) * leaf_size]
        block_rows = leaf_rows[leaf_half * leaf_size : (leaf_half + 1) * leaf_size]
        dense_block = kernel(block_pts, block_pts).astype(jnp.bfloat16)
        leaf_parts.append(jnp.dot(dense_block, block_rows, preferred_element_type=jnp.float32))
        basis_block = kernel(block_pts, anchor_set[leaf_half]).astype(jnp.bfloat16)
        leaf_bases.append(basis_block)
        leaf_coefs.append(contract_rows(basis_block, block_rows))
    local_scale = 1.0 / math.sqrt(leaf_size)
    for leaf_half in range(2):
        mixed_coef = jnp.dot(
            core_set[leaf_half],
            leaf_coefs[1 - leaf_half] * local_scale,
            precision=lax.Precision.HIGHEST,
        )
        mixed_coef = mixed_coef.astype(jnp.bfloat16)
        leaf_parts[leaf_half] = leaf_parts[leaf_half] + jnp.dot(
            leaf_bases[leaf_half], mixed_coef, preferred_element_type=jnp.float32
        )
    result = jnp.concatenate(leaf_parts, 0) + jnp.dot(
        basis_far, far_mix, preferred_element_type=jnp.float32
    )
    return jnp.zeros_like(result).at[perm_rows].set(result)


def per_device(points, rhs, order, anchors, coupling):
    lo_bits = lax.axis_size("lo").bit_length() - 1
    hi_bits = lax.axis_size("hi").bit_length() - 1
    perm_rows = order[0, 0]
    leaf_pts = points[0, 0][:, perm_rows]
    leaf_rows = rhs[0, 0][perm_rows]
    anchor_set = anchors[0, 0]
    core_set = coupling[0, 0]
    far_sets = anchor_set.shape[0] - 2
    rank_size = anchor_set.shape[2]
    rhs_count = leaf_rows.shape[1]
    basis_far = far_basis(leaf_pts, anchor_set)
    partials = contract_rows(basis_far, leaf_rows).reshape(far_sets, rank_size, rhs_count)
    siblings = []
    carried = partials
    for bit_pos in range(lo_bits):
        received = from_partner(carried, "lo", bit_pos)
        siblings.append(received[0])
        carried = carried[1:] + received[1:]
    upper_sums = carried
    carried = upper_sums
    for bit_pos in range(hi_bits):
        received = from_partner(carried, "hi", bit_pos)
        siblings.append(received[0])
        carried = carried[1:] + received[1:]
    sibling_coef = jnp.stack(siblings, 0)
    result = apply_device(
        leaf_pts, leaf_rows, anchor_set, core_set, sibling_coef, perm_rows, basis_far
    )
    return result[None, None]


def solution(mesh):
    return jax.shard_map(
        per_device,
        mesh=mesh,
        in_specs=(
            P("hi", "lo", None, None),
            P("hi", "lo", None, None),
            P("hi", "lo", None),
            P("hi", "lo", None, None, None),
            P("hi", "lo", None, None, None),
        ),
        out_specs=P("hi", "lo", None, None),
        check_vma=False,
    )
```

profile of v0, /device:TPU:1, one launch (start us, length us, event | category | flops | bytes accessed | tf_op | source)
XLA Modules:
  0.0 187.6 jit_solution(1462513315022735470)
XLA Ops:
  1.8 1.5 copy.8
  3.3 15.0 %gather_fusion.1 = bf16[4096,128]{1,0:T(8,128)(2,1)} fusion(bf16[4096,128]{1,0:T(8,128)(2,1)S(1)} %bitcast.56, s32[4096]{0:T(1024)S(1)} %broadcast_clamp_fusion), kind=kCustom, calls=%fused_computation.1 | custom fusion | bytes 2113536 | tf_op jit(solution)/shard_map/gather | solution.py:93
  18.4 12.1 %gather_fusion = bf16[4096,64]{1,0:T(8,128)(2,1)S(1)} fusion(bf16[64,4096]{0,1:T(8,128)(2,1)S(1)} %bitcast.57, s32[4096]{0:T(1024)S(1)} %broadcast_clamp_fusion), kind=kCustom, calls=%fused_computation | custom fusion | bytes 1064960 | tf_op jit(solution)/shard_map/gather | solution.py:92
  31.2 4.4 %exponential_convert_fusion = bf16[4096,1152]{1,0:T(8,128)(2,1)S(1)} fusion(bf16[4096,64]{1,0:T(8,128)(2,1)S(1)} %gather_fusion, f32[1152]{0:T(1024)S(1)} %bitcast.67, f32[4096]{0:T(1024)S(1)} %multiply_reduce_fusion, bf16[1,1,11,64,128]{4,3,2,1,0:T(8,128)(2,1)S(1)} %copy-done.6), kind=kOutput, calls=%fused_computation.5 | convolution fusion | flops 627572736 | bytes 10657792 | tf_op jit(solution)/shard_map/dot_general | solution.py:20
  35.6 3.6 %copy-done.1 = bf16[4096,1152]{1,0:T(8,128)(2,1)} copy-done((bf16[4096,1152]{1,0:T(8,128)(2,1)}, bf16[4096,1152]{1,0:T(8,128)(2,1)S(1)}, u32[]{:S(2)}) %copy-start.1) | copy-done | bytes 9437208
  39.2 3.5 %fusion.41 = f32[1152,128]{1,0:T(8,128)} fusion(bf16[4096,1152]{1,0:T(8,128)(2,1)S(1)} %exponential_convert_fusion, bf16[4096,128]{1,0:T(8,128)(2,1)S(1)} %copy-done.2), kind=kOutput, calls=%fused_computation.82 | convolution fusion | flops 1207959552 | bytes 11075584 | tf_op jit(solution)/shard_map/dot_general | solution.py:43
  42.7 4.1 %collective-permute-start = (f32[9,128,128]{2,1,0:T(8,128)}, f32[9,128,128]{2,1,0:T(8,128)}, u32[]{:S(2)}, u32[]{:S(2)}) collective-permute-start(f32[9,128,128]{2,1,0:T(8,128)} %bitcast.13), channel_id=1, source_target_pairs={{0,32},{32,0},{64,96},{96,64},{128,160},{160,128},{192,224},{224,1... | collective-permute-start | bytes 1769480 | tf_op jit(solution)/shard_map/ppermute | solution.py:16
  48.6 6.6 %fusion.9 = f32[2048,128]{1,0:T(8,128)} fusion(f32[2048]{0:T(1024)S(1)} %get-tuple-element.5, bf16[4096,128]{1,0:T(8,128)(2,1)} %gather_fusion.1, bf16[64,4096]{0,1:T(8,128)(2,1)S(1)} %bitcast.59), kind=kOutput, calls=%fused_computation.21 | convolution fusion | flops 1631584256 | bytes 2113536 | tf_op jit(solution)/shard_map/dot_general | solution.py:67
  55.2 1.2 fusion.7
  56.4 6.7 %fusion.10 = f32[2048,128]{1,0:T(8,128)} fusion(f32[2048]{0:T(1024)S(1)} %get-tuple-element.6, bf16[4096,128]{1,0:T(8,128)(2,1)} %gather_fusion.1, bf16[64,4096]{0,1:T(8,128)(2,1)S(1)} %bitcast.61), kind=kOutput, calls=%fused_computation.22 | convolution fusion | flops 1631584256 | bytes 2113536 | tf_op jit(solution)/shard_map/dot_general | solution.py:67
  63.1 1.2 slice_add_fusion
  64.4 4.4 %collective-permute-start.1 = (f32[8,128,128]{2,1,0:T(8,128)S(1)}, f32[8,128,128]{2,1,0:T(8,128)S(1)}, u32[]{:S(2)}, u32[]{:S(2)}) collective-permute-start(f32[8,128,128]{2,1,0:T(8,128)S(1)} %slice_add_fusion), channel_id=1, source_target_pairs={{0,64},{64,0},{32,96},{96,32},{128,192},{192,128},{160,224},{224,1... | collective-permute-start | bytes 1572872 | tf_op jit(solution)/shard_map/ppermute | solution.py:16
  69.1 1.5 convolution_multiply_fusion.3
  70.7 1.4 convolution_multiply_fusion.4
  72.1 5.7 %collective-permute-done.1 = f32[8,128,128]{2,1,0:T(8,128)S(1)} collective-permute-done((f32[8,128,128]{2,1,0:T(8,128)S(1)}, f32[8,128,128]{2,1,0:T(8,128)S(1)}, u32[]{:S(2)}, u32[]{:S(2)}) %collective-permute-start.1) | collective-permute-done | bytes 524320 | tf_op jit(solution)/shard_map/ppermute | solution.py:16
  77.9 5.9 %collective-permute-start.2 = (f32[7,128,128]{2,1,0:T(8,128)S(1)}, f32[7,128,128]{2,1,0:T(8,128)S(1)}, u32[]{:S(2)}, u32[]{:S(2)}) collective-permute-start(f32[7,128,128]{2,1,0:T(8,128)S(1)} %slice_add_fusion.1), channel_id=1, source_target_pairs={{0,128},{128,0},{32,160},{160,32},{64,192},{192,64},{96,224},{224,... | collective-permute-start | bytes 1376264 | tf_op jit(solution)/shard_map/ppermute | solution.py:16
  84.0 1.5 convolution_add_fusion.1
  85.6 6.5 %collective-permute-done.2 = f32[7,128,128]{2,1,0:T(8,128)S(1)} collective-permute-done((f32[7,128,128]{2,1,0:T(8,128)S(1)}, f32[7,128,128]{2,1,0:T(8,128)S(1)}, u32[]{:S(2)}, u32[]{:S(2)}) %collective-permute-start.2) | collective-permute-done | bytes 458784 | tf_op jit(solution)/shard_map/ppermute | solution.py:16
  92.1 5.1 %collective-permute-start.3 = (f32[6,128,128]{2,1,0:T(8,128)S(1)}, f32[6,128,128]{2,1,0:T(8,128)S(1)}, u32[]{:S(2)}, u32[]{:S(2)}) collective-permute-start(f32[6,128,128]{2,1,0:T(8,128)S(1)} %slice_add_fusion.2), channel_id=1, source_target_pairs={{0,256},{256,0},{32,288},{288,32},{64,320},{320,64},{96,352},{352,... | collective-permute-start | bytes 1179656 | tf_op jit(solution)/shard_map/ppermute | solution.py:16
  98.3 5.3 %collective-permute-done.3 = f32[6,128,128]{2,1,0:T(8,128)S(1)} collective-permute-done((f32[6,128,128]{2,1,0:T(8,128)S(1)}, f32[6,128,128]{2,1,0:T(8,128)S(1)}, u32[]{:S(2)}, u32[]{:S(2)}) %collective-permute-start.3) | collective-permute-done | bytes 393248 | tf_op jit(solution)/shard_map/ppermute | solution.py:16
  103.6 5.5 %collective-permute-start.4 = (f32[5,128,128]{2,1,0:T(8,128)S(1)}, f32[5,128,128]{2,1,0:T(8,128)S(1)}, u32[]{:S(2)}, u32[]{:S(2)}) collective-permute-start(f32[5,128,128]{2,1,0:T(8,128)S(1)} %slice_add_fusion.3), channel_id=1, source_target_pairs={{0,1},{1,0},{2,3},{3,2},{4,5},{5,4},{6,7},{7,6},{8,9},{9,8},{10,11... | collective-permute-start | bytes 983048 | tf_op jit(solution)/shard_map/ppermute | solution.py:16
  109.2 1.2 collective-permute-done.4
  110.5 3.6 %collective-permute-start.5 = (f32[4,128,128]{2,1,0:T(8,128)S(1)}, f32[4,128,128]{2,1,0:T(8,128)S(1)}, u32[]{:S(2)}, u32[]{:S(2)}) collective-permute-start(f32[4,128,128]{2,1,0:T(8,128)S(1)} %slice_add_fusion.4), channel_id=1, source_target_pairs={{0,2},{2,0},{1,3},{3,1},{4,6},{6,4},{5,7},{7,5},{8,10},{10,8},{9,1... | collective-permute-start | bytes 786440 | tf_op jit(solution)/shard_map/ppermute | solution.py:16
  114.1 6.3 %collective-permute-done.5 = f32[4,128,128]{2,1,0:T(8,128)S(1)} collective-permute-done((f32[4,128,128]{2,1,0:T(8,128)S(1)}, f32[4,128,128]{2,1,0:T(8,128)S(1)}, u32[]{:S(2)}, u32[]{:S(2)}) %collective-permute-start.5) | collective-permute-done | bytes 262176 | tf_op jit(solution)/shard_map/ppermute | solution.py:16
  120.4 4.8 %collective-permute-start.6 = (f32[3,128,128]{2,1,0:T(8,128)S(1)}, f32[3,128,128]{2,1,0:T(8,128)S(1)}, u32[]{:S(2)}, u32[]{:S(2)}) collective-permute-start(f32[3,128,128]{2,1,0:T(8,128)S(1)} %slice_add_fusion.5), channel_id=1, source_target_pairs={{0,4},{4,0},{1,5},{5,1},{2,6},{6,2},{3,7},{7,3},{8,12},{12,8},{9,1... | collective-permute-start | bytes 589832 | tf_op jit(solution)/shard_map/ppermute | solution.py:16
  125.3 8.6 %collective-permute-done.6 = f32[3,128,128]{2,1,0:T(8,128)S(1)} collective-permute-done((f32[3,128,128]{2,1,0:T(8,128)S(1)}, f32[3,128,128]{2,1,0:T(8,128)S(1)}, u32[]{:S(2)}, u32[]{:S(2)}) %collective-permute-start.6) | collective-permute-done | bytes 196640 | tf_op jit(solution)/shard_map/ppermute | solution.py:16
  133.9 8.8 %collective-permute-start.7 = (f32[2,128,128]{2,1,0:T(8,128)S(1)}, f32[2,128,128]{2,1,0:T(8,128)S(1)}, u32[]{:S(2)}, u32[]{:S(2)}) collective-permute-start(f32[2,128,128]{2,1,0:T(8,128)S(1)} %slice_add_fusion.6), channel_id=1, source_target_pairs={{0,8},{8,0},{1,9},{9,1},{2,10},{10,2},{3,11},{11,3},{4,12},{12,4},... | collective-permute-start | bytes 393224 | tf_op jit(solution)/shard_map/ppermute | solution.py:16
  142.8 11.2 %collective-permute-done.7 = f32[2,128,128]{2,1,0:T(8,128)S(1)} collective-permute-done((f32[2,128,128]{2,1,0:T(8,128)S(1)}, f32[2,128,128]{2,1,0:T(8,128)S(1)}, u32[]{:S(2)}, u32[]{:S(2)}) %collective-permute-start.7) | collective-permute-done | bytes 131104 | tf_op jit(solution)/shard_map/ppermute | solution.py:16
  154.0 13.0 %collective-permute-start.8 = (f32[1,128,128]{2,1,0:T(8,128)S(1)}, f32[1,128,128]{2,1,0:T(8,128)S(1)}, u32[]{:S(2)}, u32[]{:S(2)}) collective-permute-start(f32[1,128,128]{2,1,0:T(8,128)S(1)} %get-tuple-element.9), channel_id=1, source_target_pairs={{0,16},{16,0},{1,17},{17,1},{2,18},{18,2},{3,19},{19,3},{4,20},{20... | collective-permute-start | bytes 196616 | tf_op jit(solution)/shard_map/ppermute | solution.py:16
  167.3 1.7 collective-permute-done.8
  169.8 5.8 %convolution_add_fusion = f32[4096,128]{1,0:T(8,128)S(1)} fusion(bf16[4096,1152]{1,0:T(8,128)(2,1)} %copy-done.1, bf16[1152,128]{1,0:T(8,128)(2,1)S(1)} %bitcast.64, f32[2048,128]{1,0:T(8,128)S(1)} %convolution_add_fusion.1, f32[2048,128]{1,0:T(8,128)S(1)} %convolution_add_fusion.2), kind=kOutput, calls=%fused_computation.8 | convolution fusion | flops 1209008128 | bytes 13926400 | tf_op jit(solution)/shard_map/dot_general | solution.py:82
  175.6 12.0 %scatter_custom_fusion = f32[4096,128]{1,0:T(8,128)} fusion(s32[4096]{0:T(1024)S(1)} %bitcast.66, f32[4096,128]{1,0:T(8,128)S(1)} %convolution_add_fusion, f32[]{:T(128)} %constant.7.clone.1), kind=kCustom, calls=%fused_computation.31 | custom fusion | bytes 2097156 | tf_op jit(solution)/shard_map/scatter | solution.py:85
  (43 shorter events, 7.3 us)
Async XLA Ops:
  0.0 3.3 %copy-start = (bf16[1,1,4096,128]{3,2,1,0:T(8,128)(2,1)S(1)}, bf16[1,1,4096,128]{3,2,1,0:T(8,128)(2,1)}, u32[]{:S(2)}) copy-start(bf16[1,1,4096,128]{3,2,1,0:T(8,128)(2,1)} %param.7) | copy-start | bytes 3145732
  0.0 31.1 %copy-start.6 = (bf16[1,1,11,64,128]{4,3,2,1,0:T(8,128)(2,1)S(1)}, bf16[1,1,11,64,128]{4,3,2,1,0:T(8,128)(2,1)}, u32[]{:S(2)}) copy-start(bf16[1,1,11,64,128]{4,3,2,1,0:T(8,128)(2,1)} %param.9) | copy-start | bytes 540676
  31.1 8.1 %copy-start.2 = (bf16[4096,128]{1,0:T(8,128)(2,1)S(1)}, bf16[4096,128]{1,0:T(8,128)(2,1)}, u32[]{:S(2)}) copy-start(bf16[4096,128]{1,0:T(8,128)(2,1)} %gather_fusion.1) | copy-start | bytes 3145732
  35.6 3.6 %copy-start.1 = (bf16[4096,1152]{1,0:T(8,128)(2,1)}, bf16[4096,1152]{1,0:T(8,128)(2,1)S(1)}, u32[]{:S(2)}) copy-start(bf16[4096,1152]{1,0:T(8,128)(2,1)S(1)} %exponential_convert_fusion) | copy-start | bytes 28311556
  42.7 20.4 %collective-permute-start = (f32[9,128,128]{2,1,0:T(8,128)}, f32[9,128,128]{2,1,0:T(8,128)}, u32[]{:S(2)}, u32[]{:S(2)}) collective-permute-start(f32[9,128,128]{2,1,0:T(8,128)} %bitcast.13), channel_id=1, source_target_pairs={{0,32},{32,0},{64,96},{96,64},{128,160},{160,128},{192,224},{224,1... | collective-permute-start | bytes 1769480 | tf_op jit(solution)/shard_map/ppermute | solution.py:16
  56.4 27.3 %copy-start.4 = (f32[1,1,11,128,128]{4,3,2,1,0:T(8,128)S(1)}, f32[1,1,11,128,128]{4,3,2,1,0:T(8,128)}, u32[]{:S(2)}) copy-start(f32[1,1,11,128,128]{4,3,2,1,0:T(8,128)} %param.10) | copy-start | bytes 2162692
  63.1 103.9 %copy-start.3 = (f32[2048,128]{1,0:T(8,128)S(1)}, f32[2048,128]{1,0:T(8,128)}, u32[]{:S(2)}) copy-start(f32[2048,128]{1,0:T(8,128)} %fusion.9) | copy-start | bytes 3145732
  63.1 103.9 %copy-start.5 = (bf16[2048,128]{1,0:T(8,128)(2,1)S(1)}, bf16[2048,128]{1,0:T(8,128)(2,1)}, u32[]{:S(2)}) copy-start(bf16[2048,128]{1,0:T(8,128)(2,1)} %fusion.7) | copy-start | bytes 1572868
  63.1 105.9 %copy-start.7 = (f32[9]{0:T(128)S(1)}, f32[9]{0:T(128)}, u32[]{:S(2)}) copy-start(f32[9]{0:T(128)} %constant.2.clone) | copy-start | bytes 112
  64.4 13.4 %collective-permute-start.1 = (f32[8,128,128]{2,1,0:T(8,128)S(1)}, f32[8,128,128]{2,1,0:T(8,128)S(1)}, u32[]{:S(2)}, u32[]{:S(2)}) collective-permute-start(f32[8,128,128]{2,1,0:T(8,128)S(1)} %slice_add_fusion), channel_id=1, source_target_pairs={{0,64},{64,0},{32,96},{96,32},{128,192},{192,128},{160,224},{224,1... | collective-permute-start | bytes 1572872 | tf_op jit(solution)/shard_map/ppermute | solution.py:16
  77.9 14.2 %collective-permute-start.2 = (f32[7,128,128]{2,1,0:T(8,128)S(1)}, f32[7,128,128]{2,1,0:T(8,128)S(1)}, u32[]{:S(2)}, u32[]{:S(2)}) collective-permute-start(f32[7,128,128]{2,1,0:T(8,128)S(1)} %slice_add_fusion.1), channel_id=1, source_target_pairs={{0,128},{128,0},{32,160},{160,32},{64,192},{192,64},{96,224},{224,... | collective-permute-start | bytes 1376264 | tf_op jit(solution)/shard_map/ppermute | solution.py:16
  92.1 11.5 %collective-permute-start.3 = (f32[6,128,128]{2,1,0:T(8,128)S(1)}, f32[6,128,128]{2,1,0:T(8,128)S(1)}, u32[]{:S(2)}, u32[]{:S(2)}) collective-permute-start(f32[6,128,128]{2,1,0:T(8,128)S(1)} %slice_add_fusion.2), channel_id=1, source_target_pairs={{0,256},{256,0},{32,288},{288,32},{64,320},{320,64},{96,352},{352,... | collective-permute-start | bytes 1179656 | tf_op jit(solution)/shard_map/ppermute | solution.py:16
  103.6 6.8 %collective-permute-start.4 = (f32[5,128,128]{2,1,0:T(8,128)S(1)}, f32[5,128,128]{2,1,0:T(8,128)S(1)}, u32[]{:S(2)}, u32[]{:S(2)}) collective-permute-start(f32[5,128,128]{2,1,0:T(8,128)S(1)} %slice_add_fusion.3), channel_id=1, source_target_pairs={{0,1},{1,0},{2,3},{3,2},{4,5},{5,4},{6,7},{7,6},{8,9},{9,8},{10,11... | collective-permute-start | bytes 983048 | tf_op jit(solution)/shard_map/ppermute | solution.py:16
  110.5 10.0 %collective-permute-start.5 = (f32[4,128,128]{2,1,0:T(8,128)S(1)}, f32[4,128,128]{2,1,0:T(8,128)S(1)}, u32[]{:S(2)}, u32[]{:S(2)}) collective-permute-start(f32[4,128,128]{2,1,0:T(8,128)S(1)} %slice_add_fusion.4), channel_id=1, source_target_pairs={{0,2},{2,0},{1,3},{3,1},{4,6},{6,4},{5,7},{7,5},{8,10},{10,8},{9,1... | collective-permute-start | bytes 786440 | tf_op jit(solution)/shard_map/ppermute | solution.py:16
  120.4 13.4 %collective-permute-start.6 = (f32[3,128,128]{2,1,0:T(8,128)S(1)}, f32[3,128,128]{2,1,0:T(8,128)S(1)}, u32[]{:S(2)}, u32[]{:S(2)}) collective-permute-start(f32[3,128,128]{2,1,0:T(8,128)S(1)} %slice_add_fusion.5), channel_id=1, source_target_pairs={{0,4},{4,0},{1,5},{5,1},{2,6},{6,2},{3,7},{7,3},{8,12},{12,8},{9,1... | collective-permute-start | bytes 589832 | tf_op jit(solution)/shard_map/ppermute | solution.py:16
  133.9 20.1 %collective-permute-start.7 = (f32[2,128,128]{2,1,0:T(8,128)S(1)}, f32[2,128,128]{2,1,0:T(8,128)S(1)}, u32[]{:S(2)}, u32[]{:S(2)}) collective-permute-start(f32[2,128,128]{2,1,0:T(8,128)S(1)} %slice_add_fusion.6), channel_id=1, source_target_pairs={{0,8},{8,0},{1,9},{9,1},{2,10},{10,2},{3,11},{11,3},{4,12},{12,4},... | collective-permute-start | bytes 393224 | tf_op jit(solution)/shard_map/ppermute | solution.py:16
  154.0 15.1 %collective-permute-start.8 = (f32[1,128,128]{2,1,0:T(8,128)S(1)}, f32[1,128,128]{2,1,0:T(8,128)S(1)}, u32[]{:S(2)}, u32[]{:S(2)}) collective-permute-start(f32[1,128,128]{2,1,0:T(8,128)S(1)} %get-tuple-element.9), channel_id=1, source_target_pairs={{0,16},{16,0},{1,17},{17,1},{2,18},{18,2},{3,19},{19,3},{4,20},{20... | collective-permute-start | bytes 196616 | tf_op jit(solution)/shard_map/ppermute | solution.py:16
where the time goes:
time: 189 us; the launch traced here: 188 us
  starting transfers between devices  55.3 us (29%)
  waiting for transfers between devices  46.4 us (25%)
  local copies, waits for them, and re-layouts  46.3 us (24%)
  matrix products  34.7 us (18%)
  other arithmetic  4.47 us (2%)
    ppermute x9, starting transfers between devices, from_partner(): return lax.ppermute(block, axis, route)  55.3 us
    ppermute x9, waiting for transfers between devices, from_partner(): return lax.ppermute(block, axis, route)  46.4 us
    gather x1, local copies, waits for them, and re-layouts, per_device(): leaf_rows = rhs[0, 0][perm_rows]  15 us
    dot_general x2, matrix products, apply_device(): jnp.dot(dense_block, block_rows, preferred_element_type=jnp.float32)  13.4 us
    gather x1, local copies, waits for them, and re-layouts, per_device(): leaf_pts = points[0, 0][:, perm_rows]  12.1 us
    scatter x1, local copies, waits for them, and re-layouts, apply_device(): return jnp.zeros_like(result).at[perm_rows].set(result)  12 us
    dot_general x3, matrix products, contract_rows(): lax.dot_general(basis_block, row_block, (((0,), (0,)), ((), ())), preferr...  6.4 us
    dot_general x3, matrix products, kernel(): lax.dot_general(left_pts, right_pts, (((0,), (0,)), ((), ())), preferred_...  6.06 us
  transfers between devices with their start and end apart: 9, of which 8 were waited for; matrix products, arithmetic and copies ran while one was open for 12% of the time, Pallas kernels for 0%

commit v1 on v0

v1 whole, which is shorter than its diff:
```python
import functools
import math

import jax
import jax.numpy as jnp
from jax import lax
from jax.experimental import pallas as pl
from jax.experimental.pallas import tpu as pltpu
from jax.sharding import PartitionSpec as P

bf16 = jnp.bfloat16
f32 = jnp.float32
MESH = pl.DeviceIdType.MESH

WIDTH = 64
RANK = 128
RHS = 128
PTS = 4096
LEAF = 2048
SIDE = 4
LO = 16
UP = 5
DOWN = 4
UPW, DOWNW = UP * RANK, DOWN * RANK
FARW = UPW + DOWNW
ALLW = FARW + 2 * RANK
ROWS = RHS // LO
DEPTH = 128
EXPONENT = math.log2(math.e) * 4.0 / WIDTH
SIGN = 32.0
COLS = 1024


def dot(a, b):
    return jnp.dot(a, b, preferred_element_type=f32)


def dot_nt(a, b, **kw):
    return lax.dot_general(a, b, (((1,), (1,)), ((), ())), preferred_element_type=f32, **kw)


def gauss(a, b):
    return jnp.exp2(dot(a, b) * EXPONENT).astype(bf16)


def flip(index, mask):
    for bit in range(5):
        if mask >> bit & 1:
            step = 1 << bit
            index = index + step * (1 - 2 * (index // step % 2))
    return index


def split3(value):
    first = value.astype(bf16).astype(f32)
    rest = value - first
    second = rest.astype(bf16).astype(f32)
    return first, second, rest - second


def extended(cols, sign, offset, mirrored):
    n = cols.shape[1]
    half = -0.5 * jnp.sum(cols * cols, axis=0, keepdims=True)
    first, second, third = split3(half)
    row = lax.broadcasted_iota(jnp.int32, (16, n), 0)
    base = 3 if mirrored else 0
    block = jnp.where((row < 6), 1.0, 0.0)
    block = jnp.where(row == base, first, block)
    block = jnp.where(row == base + 1, second, block)
    block = jnp.where(row == base + 2, third, block)
    block = jnp.where(row == 6, sign, block)
    return jnp.where(row == 7, offset, block)


def body(
    points, rhs, order, anchors, coupling, out,
    xr, xlt, zlt, xt, vt, yt, tt, srow,
    pt_up, pt_down, et, rs_up, rs_down, q_up, a_in, g_up, b_in, ct_up, ct_down, ag_down,
    su_s, su_r, sd_s, sd_r, gu_s, gu_r, gd_s, gd_r, a_s, a_r, b_s, b_r,
):
    lo, hi = lax.axis_index("lo"), lax.axis_index("hi")
    y, x = lo // SIDE, lo % SIDE
    mine = pl.ds(pl.multiple_of(ROWS * lo, ROWS), ROWS)

    def at(d):
        dy, dx = d // SIDE, d % SIDE
        onward = (y + dy) % SIDE * SIDE + (x + dx) % SIDE
        back = (y + SIDE - dy) % SIDE * SIDE + (x + SIDE - dx) % SIDE
        return onward, back

    def rows_of(index):
        return pl.ds(pl.multiple_of(ROWS * index, ROWS), ROWS)

    def copy(src, dst, send, recv, where):
        return pltpu.make_async_remote_copy(
            src_ref=src, dst_ref=dst, send_sem=send, recv_sem=recv, device_id=where, device_id_type=MESH
        )

    def scatter(d, src, dst, send, recv):
        onward, _ = at(d)
        return copy(src.at[rows_of(onward)], dst.at[lo], send.at[d], recv.at[d], {"lo": onward, "hi": hi})

    def gather_up(d):
        onward, _ = at(d)
        return copy(ct_up.at[mine], ct_up.at[mine], gu_s.at[d], gu_r.at[d], {"lo": onward, "hi": hi})

    def gather_down(d):
        onward, _ = at(d)
        return copy(ag_down.at[onward], ct_down.at[mine], gd_s.at[d], gd_r.at[d], {"lo": onward, "hi": hi})

    def across_near(m):
        return copy(q_up, a_in.at[m - 1], a_s.at[m - 1], a_r.at[m - 1], {"lo": lo, "hi": flip(hi, m)})

    def across_far(m):
        level = 0 if m == 1 else 1 if m < 4 else 2
        src = g_up.at[:, level * RANK : (level + 1) * RANK]
        return copy(src, b_in.at[m - 1], b_s.at[m - 1], b_r.at[m - 1], {"lo": lo, "hi": flip(hi, 4 * m)})

    def each(fn):
        def step(d, c):
            fn(d)
            return c

        lax.fori_loop(1, LO, step, 0)

    barrier = pltpu.get_barrier_semaphore()
    each(lambda d: pl.semaphore_signal(barrier, inc=1, device_id={"lo": at(d)[0], "hi": hi}, device_id_type=MESH))
    partners = [m for m in range(1, 4)] + [4 * m for m in range(1, 8)]
    for m in partners:
        pl.semaphore_signal(barrier, inc=1, device_id={"lo": lo, "hi": flip(hi, m)}, device_id_type=MESH)

    lane_hot, row_hot = [], []
    for k in range(LEAF // 128, PTS // 128):
        line = order[k : k + 1, :]
        lane_hot.append(jnp.where(lax.broadcasted_iota(jnp.int32, (128, 128), 0) == (line & 127), 1.0, 0.0).astype(bf16))
        row_hot.append(jnp.where(lax.broadcasted_iota(jnp.int32, (32, 128), 0) == (line >> 7), 1.0, 0.0).astype(bf16))
    in_second = dot_nt(jnp.concatenate(row_hot, 1), jnp.concatenate(lane_hot, 1))
    signs = (2.0 * in_second - 1.0) * SIGN
    for k in range(PTS // 128):
        srow[:, k * 128 : (k + 1) * 128] = signs[k : k + 1, :]

    for c in range(0, PTS, COLS):
        cut = slice(c, c + COLS)
        cols = points[:, cut].astype(f32)
        xr[0:WIDTH, cut] = points[:, cut]
        xr[WIDTH : WIDTH + 16, cut] = extended(cols, srow[:, cut], 1.0, False).astype(bf16)
        xr[WIDTH + 16 : DEPTH, cut] = jnp.zeros((DEPTH - WIDTH - 16, COLS), bf16)
        left = jnp.concatenate(
            [cols, extended(cols, srow[:, cut], -SIGN * SIGN, True), jnp.zeros((DEPTH - WIDTH - 16, COLS), f32)], 0
        )
        xlt[cut, :] = left.T.astype(bf16)
        xt[:, cut] = rhs[cut, :].astype(f32).T.astype(bf16)
    sets = [2 + DOWN + j for j in range(UP)] + [2 + j for j in range(DOWN)] + [0, 1]
    for k, s in enumerate(sets):
        cols = anchors[s].astype(f32)
        sign = SIGN * (2 * s - 1) if s < 2 else 0.0
        offset = -SIGN * SIGN if s < 2 else 0.0
        left = jnp.concatenate(
            [cols, extended(cols, sign, offset, True), jnp.zeros((DEPTH - WIDTH - 16, RANK), f32)], 0
        )
        zlt[k * RANK : (k + 1) * RANK, :] = left.T.astype(bf16)

    def basis(first, width, total):
        total[...] = jnp.zeros_like(total)

        def step(i, c):
            cut = pl.ds(pl.multiple_of(i * LEAF, LEAF), LEAF)
            tile = gauss(zlt[first : first + width], xr[:, cut])
            vt[first : first + width, cut] = tile
            total[...] += dot_nt(xt[:, cut], tile)
            return c

        lax.fori_loop(0, PTS // LEAF, step, 0)

    basis(0, UPW, pt_up)
    pl.semaphore_wait(barrier, LO - 1 + len(partners))
    each(lambda d: scatter(d, pt_up, rs_up, su_s, su_r).start())
    rs_up[lo] = pt_up[mine, :]
    basis(UPW, DOWNW, pt_down)
    each(lambda d: scatter(d, pt_down, rs_down, sd_s, sd_r).start())
    rs_down[lo] = pt_down[mine, :]
    basis(FARW, 2 * RANK, et)

    def mix(coef, core, scale):
        return dot_nt(coef * scale, core, precision=lax.Precision.HIGHEST).astype(bf16)

    for a in range(2):
        coef = et[:, (1 - a) * RANK : (2 - a) * RANK]
        tt[:, FARW + a * RANK : FARW + (a + 1) * RANK] = mix(coef, coupling[a], 1.0 / math.sqrt(LEAF))

    def near_sums():
        each(lambda d: scatter(d, pt_up, rs_up, su_s, su_r).wait_recv())
        total = rs_up[0]
        for g in range(1, LO):
            total = total + rs_up[g]
        q_up[...] = total
        for m in range(1, 4):
            across_near(m).start()

    def far_sums():
        for m in range(1, 4):
            across_near(m).wait_recv()
        lanes = slice(2 * RANK, UPW)
        g_up[...] = (q_up[:, lanes] + a_in[0, :, lanes]) + (a_in[1, :, lanes] + a_in[2, :, lanes])
        for m in range(1, 8):
            across_far(m).start()
        ct_up[mine, 0:RANK] = a_in[0, :, 0:RANK]
        ct_up[mine, RANK : 2 * RANK] = a_in[1, :, RANK : 2 * RANK] + a_in[2, :, RANK : 2 * RANK]

    def send_down():
        each(lambda d: scatter(d, pt_down, rs_down, sd_s, sd_r).wait_recv())
        for j in range(DOWN):
            lanes = slice(j * RANK, (j + 1) * RANK)
            sums = [rs_down[g, :, lanes] for g in range(LO)]
            for _ in range(j):
                sums = [sums[2 * k] + sums[2 * k + 1] for k in range(len(sums) // 2)]
            for g in range(LO):
                ag_down[g, :, lanes] = sums[(g >> j) ^ 1]
        each(lambda d: gather_down(d).start())
        ct_down[mine, :] = ag_down[lo]

    def send_up():
        for m in range(1, 8):
            across_far(m).wait_recv()
        ct_up[mine, 2 * RANK : 3 * RANK] = b_in[0]
        ct_up[mine, 3 * RANK : 4 * RANK] = b_in[1] + b_in[2]
        ct_up[mine, 4 * RANK : 5 * RANK] = (b_in[3] + b_in[4]) + (b_in[5] + b_in[6])
        each(lambda d: gather_up(d).start())

    def dense(i, c):
        cut = pl.ds(pl.multiple_of(i * COLS, COLS), COLS)
        right = xr[:, cut]
        total = dot(tt[:, FARW:ALLW], vt[FARW:ALLW, cut])
        for r in range(0, PTS, COLS):
            total = total + dot(xt[:, r : r + COLS], gauss(xlt[r : r + COLS, :], right))
        yt[:, cut] = total

        @pl.when(i == 0)
        def _():
            near_sums()

        @pl.when(i == 1)
        def _():
            far_sums()
            send_down()

        @pl.when(i == 2)
        def _():
            send_up()

        return c

    lax.fori_loop(0, PTS // COLS, dense, 0)

    each(lambda d: gather_down(d).wait_recv())
    for j in range(DOWN):
        scale = 1.0 / math.sqrt(PTS * 2.0**j)
        lanes = slice(j * RANK, (j + 1) * RANK)
        tt[:, UPW + j * RANK : UPW + (j + 1) * RANK] = mix(ct_down[:, lanes], coupling[2 + j], scale)
    each(lambda d: gather_up(d).wait_recv())
    for j in range(UP):
        scale = 1.0 / math.sqrt(PTS * 2.0 ** (DOWN + j))
        lanes = slice(j * RANK, (j + 1) * RANK)
        tt[:, lanes] = mix(ct_up[:, lanes], coupling[2 + DOWN + j], scale)
    for c in range(0, PTS, COLS):
        cut = slice(c, c + COLS)
        out[cut, :] = (yt[:, cut] + dot(tt[:, 0:FARW], vt[0:FARW, cut])).T

    each(lambda d: scatter(d, pt_up, rs_up, su_s, su_r).wait_send())
    each(lambda d: scatter(d, pt_down, rs_down, sd_s, sd_r).wait_send())
    each(lambda d: gather_up(d).wait_send())
    each(lambda d: gather_down(d).wait_send())
    for m in range(1, 4):
        across_near(m).wait_send()
    for m in range(1, 8):
        across_far(m).wait_send()


def per_device(points, rhs, order, anchors, coupling):
    vmem = pl.BlockSpec(memory_space=pltpu.VMEM)
    scratch = [
        ((DEPTH, PTS), bf16),
        ((PTS, DEPTH), bf16),
        ((ALLW, DEPTH), bf16),
        ((RHS, PTS), bf16),
        ((ALLW, PTS), bf16),
        ((RHS, PTS), f32),
        ((RHS, ALLW), bf16),
        ((1, PTS), f32),
        ((RHS, UPW), f32),
        ((RHS, DOWNW), f32),
        ((RHS, 2 * RANK), f32),
        ((LO, ROWS, UPW), f32),
        ((LO, ROWS, DOWNW), f32),
        ((ROWS, UPW), f32),
        ((3, ROWS, UPW), f32),
        ((ROWS, 3 * RANK), f32),
        ((7, ROWS, RANK), f32),
        ((RHS, UPW), f32),
        ((RHS, DOWNW), f32),
        ((LO, ROWS, DOWNW), f32),
    ]
    sems = [pltpu.SemaphoreType.DMA((LO,))] * 8 + [pltpu.SemaphoreType.DMA((3,))] * 2 + [pltpu.SemaphoreType.DMA((7,))] * 2
    out = pl.pallas_call(
        body,
        out_shape=jax.ShapeDtypeStruct((PTS, RHS), f32),
        in_specs=[vmem] * 5,
        out_specs=vmem,
        scratch_shapes=[pltpu.VMEM(s, d) for s, d in scratch] + sems,
        compiler_params=pltpu.CompilerParams(
            collective_id=0, has_side_effects=True, vmem_limit_bytes=56 * 2**20
        ),
        name="hodlr",
    )(points[0, 0], rhs[0, 0], order[0, 0].reshape(PTS // 128, 128), anchors[0, 0], coupling[0, 0])
    return out[None, None]


def solution(mesh):
    return jax.shard_map(
        per_device,
        mesh=mesh,
        in_specs=(
            P("hi", "lo", None, None),
            P("hi", "lo", None, None),
            P("hi", "lo", None),
            P("hi", "lo", None, None, None),
            P("hi", "lo", None, None, None),
        ),
        out_specs=P("hi", "lo", None, None),
        check_vma=False,
    )
```

time: 189 us -> 51.5 us (0.27)
  starting transfers between devices: 55.3 us -> 0 us
  Pallas kernels: 0 us -> 48.3 us
  waiting for transfers between devices: 46.4 us -> 0 us
  local copies, waits for them, and re-layouts: 46.3 us -> 3.05 us
  matrix products: 34.7 us -> 0 us
  other arithmetic: 4.47 us -> 0 us
    ppermute x9 -> x0, starting transfers between devices: 55.3 us -> none  [from_partner(): return lax.ppermute(block, axis, route)]
    pallas_call x0 -> x1, Pallas kernels: none -> 48.3 us  [per_device(): pl.pallas_call(body, out_shape=jax.ShapeDtypeStruct((PTS, RHS), f32), in_...]
    ppermute x9 -> x0, waiting for transfers between devices: 46.4 us -> none  [from_partner(): return lax.ppermute(block, axis, route)]
    dot_general x14 -> x0, matrix products: 34.7 us -> none  [the longest x2 13.4 us: apply_device(): jnp.dot(dense_block, block_rows, preferred_element_type=jnp.float32)]
    gather x2 -> x0, local copies, waits for them, and re-layouts: 27.2 us -> none  [the longest x1 15 us: per_device(): leaf_rows = rhs[0, 0][perm_rows]]
    scatter x1 -> x0, local copies, waits for them, and re-layouts: 12 us -> none  [apply_device(): return jnp.zeros_like(result).at[perm_rows].set(result)]
    unnamed x24 -> x1, local copies, waits for them, and re-layouts: 6.05 us -> 3.05 us
    reduce_sum x4 -> x0, other arithmetic: 2.31 us -> none  [the longest x2 1.23 us: kernel(): jnp.sum(left_wide * left_wide, 0)[:, None]]
  transfers between devices with their start and end apart: 9 -> 0, of which waited for: 8 -> 0; matrix products, arithmetic and copies ran while one was open for 12% -> 0% of each run, Pallas kernels for 0% -> 0%
where the time goes in v1:
time: 51.5 us; the launch traced here: 51.3 us
  Pallas kernels  48.3 us (94%)
  local copies, waits for them, and re-layouts  3.05 us (6%)
    pallas_call x1, Pallas kernels, per_device(): pl.pallas_call(body, out_shape=jax.ShapeDtypeStruct((PTS, RHS), f32), in_...  48.3 us
    unnamed x1, local copies, waits for them, and re-layouts  3.05 us

profile of v1, /device:TPU:1, one launch (start us, length us, event | category | flops | bytes accessed | tf_op | source)
XLA Modules:
  0.0 51.3 jit_solution(1557794294590077656)
XLA Ops:
  0.0 48.3 %hodlr.1 = f32[4096,128]{1,0:T(8,128)} custom-call(bf16[64,4096]{1,0:T(8,128)(2,1)} %bitcast.9, bf16[4096,128]{1,0:T(8,128)(2,1)} %bitcast.7, s32[32,128]{1,0:T(8,128)} %bitcast.11, bf16[11,64,128]{2,1,0:T(8,128)(2,1)} %bitcast.10, f32[11,128,128]{2,1,0:T(8,128)} %bitcast.8), custom_call_target="tpu_custom_call" | custom-call | tf_op jit(solution)/shard_map/hodlr/pallas_call | solution.py:304
  48.3 3.0 %copy.7 = f32[1,1,4096,128]{3,2,1,0:T(8,128)} copy(f32[1,1,4096,128]{3,2,1,0:T(8,128)} %bitcast.6) | data formatting | bytes 4194304

commit v2 on v1

v2 whole, which is shorter than its diff:
```python
import math

import jax
import jax.numpy as jnp
from jax import lax
from jax.experimental import pallas as pl
from jax.experimental.pallas import tpu as pltpu
from jax.sharding import PartitionSpec as P

bf16 = jnp.bfloat16
f32 = jnp.float32
MESH = pl.DeviceIdType.MESH

WIDTH = 64
RANK = 128
RHS = 128
PTS = 4096
LEAF = 2048
SIDE = 4
LO = 16
FIRST = 6
TOP, LOW = 3, 6
INSIDE = 4
TOPW, LOWW = TOP * RANK, LOW * RANK
FARW = TOPW + LOWW
ALLW = FARW + 2 * RANK
ROWS = RHS // LO
DEPTH = 128
EXPONENT = math.log2(math.e) * 4.0 / WIDTH
SIGN = 32.0
COLS = 1024
STEP = 512
SEND_NEAR, SEND_LOW, SEND_TOP = 0, 1, 5


def dot(a, b):
    return jnp.dot(a, b, preferred_element_type=f32)


def dot_nt(a, b, **kw):
    return lax.dot_general(a, b, (((1,), (1,)), ((), ())), preferred_element_type=f32, **kw)


def gauss(a, b):
    return jnp.exp2(dot(a, b) * EXPONENT).astype(bf16)


def flip(index, mask):
    for bit in range(5):
        if mask >> bit & 1:
            step = 1 << bit
            index = index + step * (1 - 2 * (index // step % 2))
    return index


def split3(value):
    first = value.astype(bf16).astype(f32)
    rest = value - first
    second = rest.astype(bf16).astype(f32)
    return first, second, rest - second


def extended(cols, sign, offset, mirrored):
    n = cols.shape[1]
    half = -0.5 * jnp.sum(cols * cols, axis=0, keepdims=True)
    first, second, third = split3(half)
    row = lax.broadcasted_iota(jnp.int32, (16, n), 0)
    base = 3 if mirrored else 0
    block = jnp.where((row < 6), 1.0, 0.0)
    block = jnp.where(row == base, first, block)
    block = jnp.where(row == base + 1, second, block)
    block = jnp.where(row == base + 2, third, block)
    block = jnp.where(row == 6, sign, block)
    return jnp.where(row == 7, offset, block)


def body(
    points_in, rhs_in, order_in, anchors_in, coupling_in, out,
    points, rhs, order, anchors, coupling,
    xr, xlt, zlt, xt, vt, yt, tt, srow,
    pt_top, pt_low, et, rs_top, rs_low, q_top, q_low, a_in, e_in, g_top, b_in, ct_top, ct_low, ag_low,
    in_s, su_s, su_r, sd_s, sd_r, gu_s, gu_r, gd_s, gd_r, a_s, a_r, e_s, e_r, b_s, b_r,
):
    arriving = [
        pltpu.make_async_copy(src, dst, in_s.at[k])
        for k, (src, dst) in enumerate(
            ((points_in, points), (anchors_in, anchors), (rhs_in, rhs), (order_in, order), (coupling_in, coupling))
        )
    ]
    for piece in arriving:
        piece.start()

    lo, hi = lax.axis_index("lo"), lax.axis_index("hi")
    y, x = lo // SIDE, lo % SIDE
    mine = pl.ds(pl.multiple_of(ROWS * lo, ROWS), ROWS)

    def onward(d):
        return (y + d // SIDE) % SIDE * SIDE + (x + d % SIDE) % SIDE

    def rows_of(index):
        return pl.ds(pl.multiple_of(ROWS * index, ROWS), ROWS)

    def copy(src, dst, send, recv, where):
        return pltpu.make_async_remote_copy(
            src_ref=src, dst_ref=dst, send_sem=send, recv_sem=recv, device_id=where, device_id_type=MESH
        )

    def scatter(d, src, dst, send, recv):
        there = onward(d)
        return copy(src.at[rows_of(there)], dst.at[lo], send.at[d], recv.at[d], {"lo": there, "hi": hi})

    def scatter_top(d):
        return scatter(d, pt_top, rs_top, su_s, su_r)

    def scatter_low(d):
        return scatter(d, pt_low, rs_low, sd_s, sd_r)

    def gather_top(d):
        return copy(ct_top.at[mine], ct_top.at[mine], gu_s.at[d], gu_r.at[d], {"lo": onward(d), "hi": hi})

    def gather_low(d):
        there = onward(d)
        return copy(ag_low.at[there], ct_low.at[mine], gd_s.at[d], gd_r.at[d], {"lo": there, "hi": hi})

    def near_top(m):
        return copy(q_top, a_in.at[m - 1], a_s.at[m - 1], a_r.at[m - 1], {"lo": lo, "hi": flip(hi, m)})

    def near_low(m):
        src = q_low.at[:, 0:RANK] if m == 1 else q_low.at[:, RANK : 2 * RANK]
        return copy(src, e_in.at[m - 1], e_s.at[m - 1], e_r.at[m - 1], {"lo": lo, "hi": flip(hi, m)})

    def far_top(m):
        level = 0 if m == 1 else 1 if m < 4 else 2
        src = g_top.at[:, level * RANK : (level + 1) * RANK]
        return copy(src, b_in.at[m - 1], b_s.at[m - 1], b_r.at[m - 1], {"lo": lo, "hi": flip(hi, 4 * m)})

    def each(fn):
        def step(d, c):
            fn(d)
            return c

        lax.fori_loop(1, LO, step, 0)

    barrier = pltpu.get_barrier_semaphore()
    each(lambda d: pl.semaphore_signal(barrier, inc=1, device_id={"lo": onward(d), "hi": hi}, device_id_type=MESH))
    partners = [m for m in range(1, 4)] + [4 * m for m in range(1, 8)]
    for m in partners:
        pl.semaphore_signal(barrier, inc=1, device_id={"lo": lo, "hi": flip(hi, m)}, device_id_type=MESH)

    pad = DEPTH - WIDTH - 16
    arriving[0].wait()
    for c in range(0, PTS, COLS):
        cut = slice(c, c + COLS)
        xr[0:WIDTH, cut] = points[:, cut]
        xr[WIDTH : WIDTH + 16, cut] = extended(points[:, cut].astype(f32), 0.0, 1.0, False).astype(bf16)
        xr[WIDTH + 16 : DEPTH, cut] = jnp.zeros((pad, COLS), bf16)

    sets = [2 + FIRST + j for j in range(TOP)] + [2 + j for j in range(LOW)] + [0, 1]

    def anchor_rows(first, last):
        for k in range(first, last):
            s = sets[k]
            cols = anchors[s].astype(f32)
            sign = SIGN * (2 * s - 1) if s < 2 else 0.0
            offset = -SIGN * SIGN if s < 2 else 0.0
            left = jnp.concatenate([cols, extended(cols, sign, offset, True), jnp.zeros((pad, RANK), f32)], 0)
            zlt[k * RANK : (k + 1) * RANK, :] = left.T.astype(bf16)

    arriving[1].wait()
    anchor_rows(0, TOP)
    arriving[2].wait()
    for c in range(0, PTS, COLS):
        cut = slice(c, c + COLS)
        xt[:, cut] = rhs[cut, :].T

    def basis(first, width, piece, sums):
        total = None
        for c in range(0, PTS, piece):
            cut = slice(c, c + piece)
            tile = gauss(zlt[first : first + width], xr[:, cut])
            vt[first : first + width, cut] = tile
            part = dot_nt(xt[:, cut], tile)
            total = part if total is None else total + part
        sums[...] = total

    basis(0, TOPW, 1024, pt_top)
    pl.semaphore_wait(barrier, LO - 1 + len(partners))
    each(lambda d: scatter_top(d).start())
    rs_top[lo] = pt_top[mine, :]
    anchor_rows(TOP, TOP + LOW)
    basis(TOPW, LOWW, 1024, pt_low)
    each(lambda d: scatter_low(d).start())
    rs_low[lo] = pt_low[mine, :]

    each(lambda d: scatter_top(d).wait_recv())
    total = rs_top[0]
    for g in range(1, LO):
        total = total + rs_top[g]
    q_top[...] = total
    for m in range(1, 4):
        near_top(m).start()

    arriving[3].wait()
    lane_hot, row_hot = [], []
    for k in range(LEAF // 128, PTS // 128):
        line = order[k : k + 1, :]
        lane_hot.append(jnp.where(lax.broadcasted_iota(jnp.int32, (128, 128), 0) == (line & 127), 1.0, 0.0).astype(bf16))
        row_hot.append(jnp.where(lax.broadcasted_iota(jnp.int32, (32, 128), 0) == (line >> 7), 1.0, 0.0).astype(bf16))
    in_second = dot_nt(jnp.concatenate(row_hot, 1), jnp.concatenate(lane_hot, 1))
    signs = (2.0 * in_second - 1.0) * SIGN
    for k in range(PTS // 128):
        srow[:, k * 128 : (k + 1) * 128] = signs[k : k + 1, :]
    for c in range(0, PTS, COLS):
        cut = slice(c, c + COLS)
        cols = points[:, cut].astype(f32)
        xr[WIDTH : WIDTH + 16, cut] = extended(cols, srow[:, cut], 1.0, False).astype(bf16)
        left = jnp.concatenate([cols, extended(cols, srow[:, cut], -SIGN * SIGN, True), jnp.zeros((pad, COLS), f32)], 0)
        xlt[cut, :] = left.T.astype(bf16)
    anchor_rows(TOP + LOW, TOP + LOW + 2)

    for m in range(1, 4):
        near_top(m).wait_recv()
    g_top[...] = (q_top[...] + a_in[0]) + (a_in[1] + a_in[2])
    for m in range(1, 8):
        far_top(m).start()

    basis(FARW, 2 * RANK, 2048, et)
    arriving[4].wait()

    def mix(coef, core, scale):
        return dot_nt(coef * scale, core, precision=lax.Precision.HIGHEST).astype(bf16)

    for a in range(2):
        coef = et[:, (1 - a) * RANK : (2 - a) * RANK]
        tt[:, FARW + a * RANK : FARW + (a + 1) * RANK] = mix(coef, coupling[a], 1.0 / math.sqrt(LEAF))

    def send_near():
        each(lambda d: scatter_low(d).wait_recv())
        lanes = slice(INSIDE * RANK, LOWW)
        total = rs_low[0, :, lanes]
        for g in range(1, LO):
            total = total + rs_low[g, :, lanes]
        q_low[...] = total
        for m in range(1, 4):
            near_low(m).start()
        for j in range(INSIDE):
            lanes = slice(j * RANK, (j + 1) * RANK)
            sums = [rs_low[g, :, lanes] for g in range(LO)]
            for _ in range(j):
                sums = [sums[2 * k] + sums[2 * k + 1] for k in range(len(sums) // 2)]
            for g in range(LO):
                ag_low[g, :, lanes] = sums[(g >> j) ^ 1]

    def send_low():
        for m in range(1, 4):
            near_low(m).wait_recv()
        fourth, fifth = e_in[0], e_in[1] + e_in[2]
        for g in range(LO):
            ag_low[g, :, INSIDE * RANK : (INSIDE + 1) * RANK] = fourth
            ag_low[g, :, (INSIDE + 1) * RANK : LOWW] = fifth
        each(lambda d: gather_low(d).start())
        ct_low[mine, :] = ag_low[lo]

    def send_top():
        for m in range(1, 8):
            far_top(m).wait_recv()
        ct_top[mine, 0:RANK] = b_in[0]
        ct_top[mine, RANK : 2 * RANK] = b_in[1] + b_in[2]
        ct_top[mine, 2 * RANK : 3 * RANK] = (b_in[3] + b_in[4]) + (b_in[5] + b_in[6])
        each(lambda d: gather_top(d).start())

    def dense(i, c):
        cut = pl.ds(pl.multiple_of(i * STEP, STEP), STEP)
        right = xr[:, cut]
        total = dot(tt[:, FARW:ALLW], vt[FARW:ALLW, cut])
        for r in range(0, PTS, LEAF):
            total = total + dot(xt[:, r : r + LEAF], gauss(xlt[r : r + LEAF, :], right))
        yt[:, cut] = total
        for when, what in ((SEND_NEAR, send_near), (SEND_LOW, send_low), (SEND_TOP, send_top)):
            pl.when(i == when)(what)
        return c

    lax.fori_loop(0, PTS // STEP, dense, 0)

    each(lambda d: gather_low(d).wait_recv())
    for j in range(LOW):
        scale = 1.0 / math.sqrt(PTS * 2.0**j)
        tt[:, TOPW + j * RANK : TOPW + (j + 1) * RANK] = mix(ct_low[:, j * RANK : (j + 1) * RANK], coupling[2 + j], scale)
    for c in range(0, PTS, LEAF):
        cut = slice(c, c + LEAF)
        yt[:, cut] += dot(tt[:, TOPW:FARW], vt[TOPW:FARW, cut])
    each(lambda d: gather_top(d).wait_recv())
    for j in range(TOP):
        scale = 1.0 / math.sqrt(PTS * 2.0 ** (FIRST + j))
        tt[:, j * RANK : (j + 1) * RANK] = mix(ct_top[:, j * RANK : (j + 1) * RANK], coupling[2 + FIRST + j], scale)
    for c in range(0, PTS, LEAF):
        cut = slice(c, c + LEAF)
        out[cut, :] = (yt[:, cut] + dot(tt[:, 0:TOPW], vt[0:TOPW, cut])).T

    each(lambda d: scatter_top(d).wait_send())
    each(lambda d: scatter_low(d).wait_send())
    each(lambda d: gather_top(d).wait_send())
    each(lambda d: gather_low(d).wait_send())
    for m in range(1, 4):
        near_top(m).wait_send()
        near_low(m).wait_send()
    for m in range(1, 8):
        far_top(m).wait_send()


def per_device(points, rhs, order, anchors, coupling):
    given = (points[0, 0], rhs[0, 0], order[0, 0].reshape(PTS // 128, 128), anchors[0, 0], coupling[0, 0])
    scratch = [(a.shape, a.dtype) for a in given] + [
        ((DEPTH, PTS), bf16),
        ((PTS, DEPTH), bf16),
        ((ALLW, DEPTH), bf16),
        ((RHS, PTS), bf16),
        ((ALLW, PTS), bf16),
        ((RHS, PTS), f32),
        ((RHS, ALLW), bf16),
        ((1, PTS), f32),
        ((RHS, TOPW), f32),
        ((RHS, LOWW), f32),
        ((RHS, 2 * RANK), f32),
        ((LO, ROWS, TOPW), f32),
        ((LO, ROWS, LOWW), f32),
        ((ROWS, TOPW), f32),
        ((ROWS, 2 * RANK), f32),
        ((3, ROWS, TOPW), f32),
        ((3, ROWS, RANK), f32),
        ((ROWS, TOPW), f32),
        ((7, ROWS, RANK), f32),
        ((RHS, TOPW), f32),
        ((RHS, LOWW), f32),
        ((LO, ROWS, LOWW), f32),
    ]
    sems = [pltpu.SemaphoreType.DMA((n,)) for n in [5] + [LO] * 8 + [3] * 4 + [7] * 2]
    out = pl.pallas_call(
        body,
        out_shape=pltpu.VMEM((PTS, RHS), f32),
        in_specs=[pl.BlockSpec(memory_space=pltpu.HBM)] * 5,
        out_specs=pl.BlockSpec(memory_space=pltpu.VMEM),
        scratch_shapes=[pltpu.VMEM(s, d) for s, d in scratch] + sems,
        compiler_params=pltpu.CompilerParams(
            collective_id=0, has_side_effects=True, vmem_limit_bytes=60 * 2**20
        ),
        name="hodlr",
    )(*given)
    return out[None, None]


def solution(mesh):
    return jax.shard_map(
        per_device,
        mesh=mesh,
        in_specs=(
            P("hi", "lo", None, None),
            P("hi", "lo", None, None),
            P("hi", "lo", None),
            P("hi", "lo", None, None, None),
            P("hi", "lo", None, None, None),
        ),
        out_specs=P("hi", "lo", None, None),
        check_vma=False,
    )
```

time: 51.5 us -> 52 us (level)
  Pallas kernels: 48.3 us -> 50.6 us
  local copies, waits for them, and re-layouts: 3.05 us -> 1.32 us
    pallas_call x1, Pallas kernels: 48.3 us -> 50.6 us  [per_device(): pl.pallas_call(body, out_shape=pltpu.VMEM((PTS, RHS), f32), in_specs=[pl....]
    unnamed x1, local copies, waits for them, and re-layouts: 3.05 us -> 1.32 us
where the time goes in v2:
time: 52 us; the launch traced here: 51.9 us
  Pallas kernels  50.6 us (97%)
  local copies, waits for them, and re-layouts  1.32 us (3%)
    pallas_call x1, Pallas kernels, per_device(): pl.pallas_call(body, out_shape=pltpu.VMEM((PTS, RHS), f32), in_specs=[pl....  50.6 us
    unnamed x1, local copies, waits for them, and re-layouts  1.32 us

profile of v2, /device:TPU:1, one launch (start us, length us, event | category | flops | bytes accessed | tf_op | source)
XLA Modules:
  0.0 51.9 jit_solution(17513104269045467288)
XLA Ops:
  0.0 50.6 %hodlr.1 = f32[4096,128]{1,0:T(8,128)S(1)} custom-call(bf16[64,4096]{1,0:T(8,128)(2,1)} %bitcast.9, bf16[4096,128]{1,0:T(8,128)(2,1)} %bitcast.7, s32[32,128]{1,0:T(8,128)} %bitcast.11, bf16[11,64,128]{2,1,0:T(8,128)(2,1)} %bitcast.10, f32[11,128,128]{2,1,0:T(8,128)} %bitcast.8), custom_call_target="tpu_custom_call" | custom-call | tf_op jit(solution)/shard_map/hodlr/pallas_call | solution.py:338
  50.6 1.3 %copy.7 = f32[1,1,4096,128]{3,2,1,0:T(8,128)} copy(f32[1,1,4096,128]{3,2,1,0:T(8,128)S(1)} %bitcast.6) | data formatting | bytes 4194304

commit v3 on v2

--- a/solution.py
+++ b/solution.py
@@ -30,7 +30,9 @@
 SIGN = 32.0
 COLS = 1024
 STEP = 512
-SEND_NEAR, SEND_LOW, SEND_TOP = 0, 1, 5
+EARLY = 2
+EARLY_AT = (2, 3, 3, 4, 6)
+LATE_AT = (-2, -1, 0, 1, 5)
 
 
 def dot(a, b):
@@ -79,7 +81,7 @@
     points, rhs, order, anchors, coupling,
     xr, xlt, zlt, xt, vt, yt, tt, srow,
     pt_top, pt_low, et, rs_top, rs_low, q_top, q_low, a_in, e_in, g_top, b_in, ct_top, ct_low, ag_low,
-    in_s, su_s, su_r, sd_s, sd_r, gu_s, gu_r, gd_s, gd_r, a_s, a_r, e_s, e_r, b_s, b_r,
+    in_s, su_s, su_r, sd_s, sd_r, gu_s, gu_r, gd_s, gd_r, a_s, a_r, e_s, e_r, b_s, b_r, ready,
 ):
     arriving = [
         pltpu.make_async_copy(src, dst, in_s.at[k])
@@ -143,9 +145,20 @@
 
     barrier = pltpu.get_barrier_semaphore()
     each(lambda d: pl.semaphore_signal(barrier, inc=1, device_id={"lo": onward(d), "hi": hi}, device_id_type=MESH))
-    partners = [m for m in range(1, 4)] + [4 * m for m in range(1, 8)]
-    for m in partners:
+    for m in range(1, 4):
         pl.semaphore_signal(barrier, inc=1, device_id={"lo": lo, "hi": flip(hi, m)}, device_id_type=MESH)
+    quad = hi // 4
+
+    def upper(m):
+        return quad // (1 << (m.bit_length() - 1)) % 2 == 1
+
+    for m in range(1, 8):
+
+        @pl.when(jnp.logical_not(upper(m)))
+        def _():
+            pl.semaphore_signal(barrier, inc=1, device_id={"lo": lo, "hi": flip(hi, 4 * m)}, device_id_type=MESH)
+
+    when_at = [jnp.where(quad < EARLY, a, b) for a, b in zip(EARLY_AT, LATE_AT)]
 
     pad = DEPTH - WIDTH - 16
     arriving[0].wait()
@@ -184,7 +197,13 @@
         sums[...] = total
 
     basis(0, TOPW, 1024, pt_top)
-    pl.semaphore_wait(barrier, LO - 1 + len(partners))
+    pl.semaphore_wait(barrier, LO - 1 + 3 + quad)
+    for m in range(1, 8):
+
+        @pl.when(upper(m))
+        def _():
+            pl.semaphore_signal(ready, inc=1, device_id={"lo": lo, "hi": flip(hi, 4 * m)}, device_id_type=MESH)
+
     each(lambda d: scatter_top(d).start())
     rs_top[lo] = pt_top[mine, :]
     anchor_rows(TOP, TOP + LOW)
@@ -192,13 +211,30 @@
     each(lambda d: scatter_low(d).start())
     rs_low[lo] = pt_low[mine, :]
 
-    each(lambda d: scatter_top(d).wait_recv())
-    total = rs_top[0]
-    for g in range(1, LO):
-        total = total + rs_top[g]
-    q_top[...] = total
-    for m in range(1, 4):
-        near_top(m).start()
+    def send_near():
+        each(lambda d: scatter_top(d).wait_recv())
+        total = rs_top[0]
+        for g in range(1, LO):
+            total = total + rs_top[g]
+        q_top[...] = total
+        for m in range(1, 4):
+            near_top(m).start()
+
+    def send_far():
+        for m in range(1, 4):
+            near_top(m).wait_recv()
+        g_top[...] = (q_top[...] + a_in[0]) + (a_in[1] + a_in[2])
+        for m in range(1, 8):
+            pl.when(upper(m))(far_top(m).start)
+
+        @pl.when(quad < 7)
+        def _():
+            pl.semaphore_wait(ready, 7 - quad)
+
+        for m in range(1, 8):
+            pl.when(jnp.logical_not(upper(m)))(far_top(m).start)
+
+    pl.when(when_at[0] == -2)(send_near)
 
     arriving[3].wait()
     lane_hot, row_hot = [], []
@@ -218,12 +254,7 @@
         xlt[cut, :] = left.T.astype(bf16)
     anchor_rows(TOP + LOW, TOP + LOW + 2)
 
-    for m in range(1, 4):
-        near_top(m).wait_recv()
-    g_top[...] = (q_top[...] + a_in[0]) + (a_in[1] + a_in[2])
-    for m in range(1, 8):
-        far_top(m).start()
-
+    pl.when(when_at[1] == -1)(send_far)
     basis(FARW, 2 * RANK, 2048, et)
     arriving[4].wait()
 
@@ -234,7 +265,7 @@
         coef = et[:, (1 - a) * RANK : (2 - a) * RANK]
         tt[:, FARW + a * RANK : FARW + (a + 1) * RANK] = mix(coef, coupling[a], 1.0 / math.sqrt(LEAF))
 
-    def send_near():
+    def sum_low():
         each(lambda d: scatter_low(d).wait_recv())
         lanes = slice(INSIDE * RANK, LOWW)
         total = rs_low[0, :, lanes]
@@ -270,14 +301,14 @@
         each(lambda d: gather_top(d).start())
 
     def dense(i, c):
+        for at, what in zip(when_at, (send_near, send_far, sum_low, send_low, send_top)):
+            pl.when(i == at)(what)
         cut = pl.ds(pl.multiple_of(i * STEP, STEP), STEP)
         right = xr[:, cut]
         total = dot(tt[:, FARW:ALLW], vt[FARW:ALLW, cut])
         for r in range(0, PTS, LEAF):
             total = total + dot(xt[:, r : r + LEAF], gauss(xlt[r : r + LEAF, :], right))
         yt[:, cut] = total
-        for when, what in ((SEND_NEAR, send_near), (SEND_LOW, send_low), (SEND_TOP, send_top)):
-            pl.when(i == when)(what)
         return c
 
     lax.fori_loop(0, PTS // STEP, dense, 0)
@@ -335,6 +366,7 @@
         ((LO, ROWS, LOWW), f32),
     ]
     sems = [pltpu.SemaphoreType.DMA((n,)) for n in [5] + [LO] * 8 + [3] * 4 + [7] * 2]
+    sems.append(pltpu.SemaphoreType.REGULAR)
     out = pl.pallas_call(
         body,
         out_shape=pltpu.VMEM((PTS, RHS), f32),

time: 52 us -> 42.7 us (0.82)
  Pallas kernels: 50.6 us -> 41.3 us
    pallas_call x1, Pallas kernels: 50.6 us -> 41.3 us  [per_device(): pl.pallas_call(body, out_shape=pltpu.VMEM((PTS, RHS), f32), in_specs=[pl....]
where the time goes in v3:
time: 42.7 us; the launch traced here: 42.6 us
  Pallas kernels  41.3 us (97%)
  local copies, waits for them, and re-layouts  1.32 us (3%)
    pallas_call x1, Pallas kernels, per_device(): pl.pallas_call(body, out_shape=pltpu.VMEM((PTS, RHS), f32), in_specs=[pl....  41.3 us
    unnamed x1, local copies, waits for them, and re-layouts  1.32 us

profile of v3, /device:TPU:1, one launch (start us, length us, event | category | flops | bytes accessed | tf_op | source)
XLA Modules:
  0.0 42.6 jit_solution(17580762864956576088)
XLA Ops:
  0.0 41.3 %hodlr.1 = f32[4096,128]{1,0:T(8,128)S(1)} custom-call(bf16[64,4096]{1,0:T(8,128)(2,1)} %bitcast.9, bf16[4096,128]{1,0:T(8,128)(2,1)} %bitcast.7, s32[32,128]{1,0:T(8,128)} %bitcast.11, bf16[11,64,128]{2,1,0:T(8,128)(2,1)} %bitcast.10, f32[11,128,128]{2,1,0:T(8,128)} %bitcast.8), custom_call_target="tpu_custom_call" | custom-call | tf_op jit(solution)/shard_map/hodlr/pallas_call | solution.py:370
  41.3 1.3 %copy.7 = f32[1,1,4096,128]{3,2,1,0:T(8,128)} copy(f32[1,1,4096,128]{3,2,1,0:T(8,128)S(1)} %bitcast.6) | data formatting | bytes 4194304

commit v4 on v3

--- a/solution.py
+++ b/solution.py
@@ -30,9 +30,15 @@
 SIGN = 32.0
 COLS = 1024
 STEP = 512
-EARLY = 2
-EARLY_AT = (2, 3, 3, 4, 6)
-LATE_AT = (-2, -1, 0, 1, 5)
+PLACES = (
+    (2, 3, 5, 3, 4, 7),
+    (1, 2, 4, 2, 3, 7),
+    (1, 2, 3, 2, 3, 6),
+    (-1, 0, 2, 1, 2, 6),
+    (-1, 0, 2, 3, 4, 6),
+    (-3, -1, 1, 2, 4, 6),
+)
+WAYS = (10, 6, 9, 11, 14, 2, 8, 5, 7, 13, 15, 1, 3, 4, 12)
 
 
 def dot(a, b):
@@ -158,7 +164,14 @@
         def _():
             pl.semaphore_signal(barrier, inc=1, device_id={"lo": lo, "hi": flip(hi, 4 * m)}, device_id_type=MESH)
 
-    when_at = [jnp.where(quad < EARLY, a, b) for a, b in zip(EARLY_AT, LATE_AT)]
+    rank = jnp.minimum(quad, 4) + jnp.where(x + y < 2, 0, jnp.where(quad == 3, 2, 1))
+    rank = jnp.where(lo + hi == 0, 3, rank)
+    places = []
+    for choice in zip(*PLACES):
+        place = choice[-1]
+        for k in range(len(choice) - 2, -1, -1):
+            place = jnp.where(rank == k, choice[k], place)
+        places.append(place)
 
     pad = DEPTH - WIDTH - 16
     arriving[0].wait()
@@ -204,13 +217,11 @@
         def _():
             pl.semaphore_signal(ready, inc=1, device_id={"lo": lo, "hi": flip(hi, 4 * m)}, device_id_type=MESH)
 
-    each(lambda d: scatter_top(d).start())
+    for d in WAYS:
+        scatter_top(d).start()
     rs_top[lo] = pt_top[mine, :]
     anchor_rows(TOP, TOP + LOW)
     basis(TOPW, LOWW, 1024, pt_low)
-    each(lambda d: scatter_low(d).start())
-    rs_low[lo] = pt_low[mine, :]
-
     def send_near():
         each(lambda d: scatter_top(d).wait_recv())
         total = rs_top[0]
@@ -227,6 +238,7 @@
         for m in range(1, 8):
             pl.when(upper(m))(far_top(m).start)
 
+    def send_up():
         @pl.when(quad < 7)
         def _():
             pl.semaphore_wait(ready, 7 - quad)
@@ -234,7 +246,10 @@
         for m in range(1, 8):
             pl.when(jnp.logical_not(upper(m)))(far_top(m).start)
 
-    pl.when(when_at[0] == -2)(send_near)
+    pl.when(places[0] == -3)(send_near)
+    start_low = lambda: each(lambda d: scatter_low(d).start())
+    pl.when(rank != 4)(start_low)
+    rs_low[lo] = pt_low[mine, :]
 
     arriving[3].wait()
     lane_hot, row_hot = [], []
@@ -254,7 +269,9 @@
         xlt[cut, :] = left.T.astype(bf16)
     anchor_rows(TOP + LOW, TOP + LOW + 2)
 
-    pl.when(when_at[1] == -1)(send_far)
+    pl.when(places[0] == -1)(send_near)
+    pl.when(rank == 4)(start_low)
+    pl.when(places[1] == -1)(send_far)
     basis(FARW, 2 * RANK, 2048, et)
     arriving[4].wait()
 
@@ -298,10 +315,11 @@
         ct_top[mine, 0:RANK] = b_in[0]
         ct_top[mine, RANK : 2 * RANK] = b_in[1] + b_in[2]
         ct_top[mine, 2 * RANK : 3 * RANK] = (b_in[3] + b_in[4]) + (b_in[5] + b_in[6])
-        each(lambda d: gather_top(d).start())
+        for d in WAYS:
+            gather_top(d).start()
 
     def dense(i, c):
-        for at, what in zip(when_at, (send_near, send_far, sum_low, send_low, send_top)):
+        for at, what in zip(places, (send_near, send_far, send_up, sum_low, send_low, send_top)):
             pl.when(i == at)(what)
         cut = pl.ds(pl.multiple_of(i * STEP, STEP), STEP)
         right = xr[:, cut]
@@ -320,6 +338,15 @@
     for c in range(0, PTS, LEAF):
         cut = slice(c, c + LEAF)
         yt[:, cut] += dot(tt[:, TOPW:FARW], vt[TOPW:FARW, cut])
+    each(lambda d: scatter_top(d).wait_send())
+    each(lambda d: scatter_low(d).wait_send())
+    each(lambda d: gather_low(d).wait_send())
+    for m in range(1, 4):
+        near_top(m).wait_send()
+        near_low(m).wait_send()
+    for m in range(1, 8):
+        far_top(m).wait_send()
+    each(lambda d: gather_top(d).wait_send())
     each(lambda d: gather_top(d).wait_recv())
     for j in range(TOP):
         scale = 1.0 / math.sqrt(PTS * 2.0 ** (FIRST + j))
@@ -327,16 +354,6 @@
     for c in range(0, PTS, LEAF):
         cut = slice(c, c + LEAF)
         out[cut, :] = (yt[:, cut] + dot(tt[:, 0:TOPW], vt[0:TOPW, cut])).T
-
-    each(lambda d: scatter_top(d).wait_send())
-    each(lambda d: scatter_low(d).wait_send())
-    each(lambda d: gather_top(d).wait_send())
-    each(lambda d: gather_low(d).wait_send())
-    for m in range(1, 4):
-        near_top(m).wait_send()
-        near_low(m).wait_send()
-    for m in range(1, 8):
-        far_top(m).wait_send()
 
 
 def per_device(points, rhs, order, anchors, coupling):

time: 42.7 us -> 41.5 us (0.972)
  Pallas kernels: 41.3 us -> 40 us
    pallas_call x1, Pallas kernels: 41.3 us -> 40 us  [per_device(): pl.pallas_call(body, out_shape=pltpu.VMEM((PTS, RHS), f32), in_specs=[pl....]
where the time goes in v4:
time: 41.5 us; the launch traced here: 41.4 us
  Pallas kernels  40 us (96%)
  local copies, waits for them, and re-layouts  1.32 us (3%)
    pallas_call x1, Pallas kernels, per_device(): pl.pallas_call(body, out_shape=pltpu.VMEM((PTS, RHS), f32), in_specs=[pl....  40 us
    unnamed x1, local copies, waits for them, and re-layouts  1.32 us

profile of v4, /device:TPU:1, one launch (start us, length us, event | category | flops | bytes accessed | tf_op | source)
XLA Modules:
  0.0 41.4 jit_solution(16372262484000745174)
XLA Ops:
  0.0 40.0 %hodlr.1 = f32[4096,128]{1,0:T(8,128)S(1)} custom-call(bf16[64,4096]{1,0:T(8,128)(2,1)} %bitcast.9, bf16[4096,128]{1,0:T(8,128)(2,1)} %bitcast.7, s32[32,128]{1,0:T(8,128)} %bitcast.11, bf16[11,64,128]{2,1,0:T(8,128)(2,1)} %bitcast.10, f32[11,128,128]{2,1,0:T(8,128)} %bitcast.8), custom_call_target="tpu_custom_call" | custom-call | tf_op jit(solution)/shard_map/hodlr/pallas_call | solution.py:387
  40.0 1.3 %copy.7 = f32[1,1,4096,128]{3,2,1,0:T(8,128)} copy(f32[1,1,4096,128]{3,2,1,0:T(8,128)S(1)} %bitcast.6) | data formatting | bytes 4194304

commit v5 on v4

--- a/solution.py
+++ b/solution.py
@@ -335,9 +335,7 @@
     for j in range(LOW):
         scale = 1.0 / math.sqrt(PTS * 2.0**j)
         tt[:, TOPW + j * RANK : TOPW + (j + 1) * RANK] = mix(ct_low[:, j * RANK : (j + 1) * RANK], coupling[2 + j], scale)
-    for c in range(0, PTS, LEAF):
-        cut = slice(c, c + LEAF)
-        yt[:, cut] += dot(tt[:, TOPW:FARW], vt[TOPW:FARW, cut])
+    yt[...] += dot(tt[:, TOPW:FARW], vt[TOPW:FARW, :])
     each(lambda d: scatter_top(d).wait_send())
     each(lambda d: scatter_low(d).wait_send())
     each(lambda d: gather_low(d).wait_send())
@@ -351,9 +349,7 @@
     for j in range(TOP):
         scale = 1.0 / math.sqrt(PTS * 2.0 ** (FIRST + j))
         tt[:, j * RANK : (j + 1) * RANK] = mix(ct_top[:, j * RANK : (j + 1) * RANK], coupling[2 + FIRST + j], scale)
-    for c in range(0, PTS, LEAF):
-        cut = slice(c, c + LEAF)
-        out[cut, :] = (yt[:, cut] + dot(tt[:, 0:TOPW], vt[0:TOPW, cut])).T
+    out[...] = (yt[...] + dot(tt[:, 0:TOPW], vt[0:TOPW, :])).T
 
 
 def per_device(points, rhs, order, anchors, coupling):

time: 41.5 us -> 41.5 us (level)
  no operation moved by 1% of the time
where the time goes in v5:
time: 41.5 us; the launch traced here: 41.4 us
  Pallas kernels  40 us (96%)
  local copies, waits for them, and re-layouts  1.32 us (3%)
    pallas_call x1, Pallas kernels, per_device(): pl.pallas_call(body, out_shape=pltpu.VMEM((PTS, RHS), f32), in_specs=[pl....  40 us
    unnamed x1, local copies, waits for them, and re-layouts  1.32 us

profile of v5, /device:TPU:1, one launch (start us, length us, event | category | flops | bytes accessed | tf_op | source)
XLA Modules:
  0.0 41.4 jit_solution(14096561434360961885)
XLA Ops:
  0.0 40.0 %hodlr.1 = f32[4096,128]{1,0:T(8,128)S(1)} custom-call(bf16[64,4096]{1,0:T(8,128)(2,1)} %bitcast.9, bf16[4096,128]{1,0:T(8,128)(2,1)} %bitcast.7, s32[32,128]{1,0:T(8,128)} %bitcast.11, bf16[11,64,128]{2,1,0:T(8,128)(2,1)} %bitcast.10, f32[11,128,128]{2,1,0:T(8,128)} %bitcast.8), custom_call_target="tpu_custom_call" | custom-call | tf_op jit(solution)/shard_map/hodlr/pallas_call | solution.py:383
  40.0 1.3 %copy.7 = f32[1,1,4096,128]{3,2,1,0:T(8,128)} copy(f32[1,1,4096,128]{3,2,1,0:T(8,128)S(1)} %bitcast.6) | data formatting | bytes 4194304
